TPU v7x, 32 devices: a whole 2x2x4 slice. The times are simulated.
32 devices in a mesh: groups: 2 (over y), row: 4 (over z), col: 4 (over x, core).
Axes of the slice: x: 2, y: 2, z: 4, core: 2. Of those that a mesh axis runs over, the one named last changes fastest.
Arguments:
- pair_act: bfloat16 [64, 32, 128], P(('groups', 'row'), 'col'), parts along dimension 0, may hold values from -6 to 6
- cotangent: bfloat16 [64, 32, 128], P(('groups', 'row'), 'col'), parts along dimension 0, may hold values from -6 to 6
- crop_len: int32 [2], P('groups'), parts along dimension 0, may hold values from 16 to 32
- ln_in_gain: float32 [128], replicated, may hold values from 0.5 to 1.5
- ln_in_bias: float32 [128], replicated, may hold values from -3 to 3
- w_left: bfloat16 [128, 256], replicated, may hold values from -0.5 to 0.5
- w_right: bfloat16 [128, 256], replicated, may hold values from -0.5 to 0.5
- w_gate: bfloat16 [128, 128], replicated, may hold values from -0.5 to 0.5
- ln_out_gain: float32 [128], replicated, may hold values from 0.5 to 1.5
- ln_out_bias: float32 [128], replicated, may hold values from -3 to 3
- w_out: bfloat16 [128, 128], replicated, may hold values from -0.5 to 0.5
Outputs:
- d_pair: bfloat16 [64, 32, 128], P(('groups', 'row'), 'col'), parts along dimension 0
There are 2 independent parts, one for each index of `groups`. A program takes and returns all parts, laid end to end along the dimension named above; an argument that names none is the same for every part. Nothing has to cross between parts.
All inputs are finite; a program needn't handle non-finite values.
Results may differ from a plain program's by a relative error of at most 0.014.
Values may be sent and summed in bfloat16 or wider, within the bound.
A program may use at most 64 MiB of HBM per device.

v0:
```python
import functools

import jax
import jax.numpy as jnp
from jax import lax
from jax.experimental import pallas as pl
from jax.experimental.pallas import tpu as pltpu
from jax.sharding import PartitionSpec as P

epsilon = 1e-05
MESH = pl.DeviceIdType.MESH


def normalize(values):
    center = jnp.mean(values, axis=-1, keepdims=True)
    shifted = values - center
    inv_std = lax.rsqrt(jnp.mean(shifted * shifted, axis=-1, keepdims=True) + epsilon)
    return (shifted * inv_std, inv_std)


def norm_back(d_scaled, scaled, inv_std):
    first = jnp.mean(d_scaled, axis=-1, keepdims=True)
    second = jnp.mean(d_scaled * scaled, axis=-1, keepdims=True)
    return inv_std * (d_scaled - first - scaled * second)


def dot(a, b):
    return jnp.dot(a, b, preferred_element_type=jnp.float32)


def dot_t(a, b):
    return lax.dot_general(a, b, (((1,), (1,)), ((), ())), preferred_element_type=jnp.float32)


def loop(count, body, init):
    if count <= 4:
        for step in range(count):
            init = body(step, init)
        return init
    return lax.fori_loop(0, count, body, init)


def each(start, count, body):
    if count <= 16:
        for step in range(start, count):
            body(step)
    else:

        @pl.loop(start, count)
        def _(step):
            body(step)


def kernel(
    n_row,
    n_col,
    rows,
    cols,
    crop_hbm,
    pair_hbm,
    cot_hbm,
    gain_in_hbm,
    bias_in_hbm,
    w_left_hbm,
    w_right_hbm,
    w_gate_hbm,
    gain_out_hbm,
    bias_out_hbm,
    w_out_hbm,
    out_ref,
    crop_ref,
    pair_ref,
    cot_ref,
    gain_in_ref,
    bias_in_ref,
    w_left_ref,
    w_right_ref,
    w_gate_ref,
    gain_out_ref,
    bias_out_ref,
    w_out_ref,
    load_in,
    left_own,
    right_own,
    turn_own,
    grad_own,
    left_row,
    right_turn,
    left_panel,
    right_panel,
    grad_row,
    grad_col,
    right_wide,
    left_wide,
    grad_row_wide,
    grad_col_wide,
    left_row_out,
    left_row_in,
    turn_out,
    turn_in,
    left_panel_out,
    left_panel_in,
    right_panel_out,
    right_panel_in,
    grad_row_out,
    grad_row_in,
    grad_col_out,
    grad_col_in,
):
    row = lax.axis_index("row")
    col = lax.axis_index("col")
    ratio = cols // rows
    cells = rows * cols
    sub = rows * rows
    width = w_out_ref.shape[0]
    home_col = row // ratio
    total = n_row * n_col

    barrier = pltpu.get_barrier_semaphore()

    def greet(step):
        other = lax.rem(row * n_col + col + step, total)
        pl.semaphore_signal(
            barrier,
            inc=1,
            device_id={"row": other // n_col, "col": lax.rem(other, n_col)},
            device_id_type=MESH,
        )

    each(1, total, greet)

    pairs = (
        (pair_hbm, pair_ref),
        (gain_in_hbm, gain_in_ref),
        (bias_in_hbm, bias_in_ref),
        (w_right_hbm, w_right_ref),
        (w_left_hbm, w_left_ref),
        (crop_hbm, crop_ref),
        (w_gate_hbm, w_gate_ref),
        (cot_hbm, cot_ref),
        (w_out_hbm, w_out_ref),
        (gain_out_hbm, gain_out_ref),
        (bias_out_hbm, bias_out_ref),
    )
    loads = [pltpu.make_async_copy(*pair, load_in.at[at]) for at, pair in enumerate(pairs)]
    for load in loads:
        load.start()

    def remote(src, dst, out_sem, in_sem, to_row, to_col):
        return pltpu.make_async_remote_copy(
            src_ref=src,
            dst_ref=dst,
            send_sem=out_sem,
            recv_sem=in_sem,
            device_id={"row": to_row, "col": to_col},
            device_id_type=MESH,
        )

    for load in loads[:6]:
        load.wait()
    position = (rows, cols, width)
    row_pos = row * rows + lax.broadcasted_iota(jnp.int32, position, 0)
    col_pos = col * cols + lax.broadcasted_iota(jnp.int32, position, 1)
    crop = crop_ref[0]
    pair_mask = jnp.where(jnp.maximum(row_pos, col_pos) < crop, 1.0, 0.0).reshape(cells, width)
    hat_in, inv_in = normalize(pair_ref[...].astype(jnp.float32))
    gain_in = gain_in_ref[...]
    normed = (hat_in * gain_in + bias_in_ref[...]).astype(jnp.bfloat16)
    right_proj = dot(normed, w_right_ref[...])
    right_lin = right_proj[:, :width]
    right_sig = jax.nn.sigmoid(right_proj[:, width:])
    right_side = (pair_mask * right_sig * right_lin).astype(jnp.bfloat16)
    right_own[...] = right_side
    right_wide[...] = right_side.astype(jnp.float32)
    turn_own[...] = jnp.concatenate(
        [right_wide[pl.ds(k, rows, stride=cols), :] for k in range(cols)], axis=0
    ).astype(jnp.bfloat16)
    left_proj = dot(normed, w_left_ref[...])
    left_lin = left_proj[:, :width]
    left_sig = jax.nn.sigmoid(left_proj[:, width:])
    left_own[...] = (pair_mask * left_sig * left_lin).astype(jnp.bfloat16)

    pl.semaphore_wait(barrier, total - 1)

    turn_slot = lax.rem(row, ratio) * n_col + col

    def turn_copy(step):
        return remote(
            turn_own,
            right_turn.at[turn_slot],
            turn_out.at[step],
            turn_in.at[turn_slot],
            lax.rem(row + step, n_row),
            home_col,
        )

    each(1, n_row, lambda step: turn_copy(step).start())

    @pl.when(home_col != col)
    def _():
        turn_copy(0).start()

    @pl.when(home_col == col)
    def _():
        pltpu.make_async_copy(turn_own, right_turn.at[turn_slot], turn_in.at[turn_slot]).start()

    def left_row_copy(step):
        return remote(
            left_own,
            left_row.at[col],
            left_row_out.at[step],
            left_row_in.at[col],
            row,
            lax.rem(col + step, n_col),
        )

    each(1, n_col, lambda step: left_row_copy(step).start())

    def right_panel_copy(step):
        return remote(
            right_own,
            right_panel.at[row],
            right_panel_out.at[step],
            right_panel_in.at[row],
            lax.rem(row + step, n_row),
            col,
        )

    def left_panel_copy(step):
        return remote(
            left_own,
            left_panel.at[row],
            left_panel_out.at[step],
            left_panel_in.at[row],
            lax.rem(row + step, n_row),
            col,
        )

    each(1, n_row, lambda step: right_panel_copy(step).start())
    each(1, n_row, lambda step: left_panel_copy(step).start())

    left_row[col] = left_own[...]
    right_panel[row] = right_own[...]
    left_panel[row] = left_own[...]

    for load in loads[6:]:
        load.wait()
    gating = jax.nn.sigmoid(dot(normed, w_gate_ref[...]))
    cot_full = cot_ref[...].astype(jnp.float32)
    d_proj = (cot_full * gating).astype(jnp.bfloat16)
    gain_out = gain_out_ref[...]
    d_scaled = dot_t(d_proj, w_out_ref[...]) * gain_out

    def arrived(buffer, sem, slot):
        remote(buffer.at[slot], buffer.at[slot], sem.at[slot], sem.at[slot], row, col).wait_recv()

    each(1, n_col, lambda step: arrived(left_row, left_row_in, lax.rem(col + step, n_col)))
    each(0, ratio * n_col, lambda slot: arrived(right_turn, turn_in, slot))

    left_wide[...] = left_row[...].astype(jnp.float32)

    def add_update(source, sums):
        sums = list(sums)
        for part in range(ratio):
            turned = right_turn[part * n_col + source].astype(jnp.float32)
            for k in range(cols):
                turned_k = turned[k * rows : (k + 1) * rows]
                for i in range(rows):
                    at = part * rows + i
                    sums[at] += left_wide[source, i * cols + k : i * cols + k + 1, :] * turned_k
        return tuple(sums)

    zero = jnp.zeros((rows, width), jnp.float32)
    sums = loop(n_col, add_update, (zero,) * (ratio * rows))
    update = jnp.concatenate(
        [sums[part * rows + i] for i in range(rows) for part in range(ratio)], axis=0
    )
    hat_out, inv_out = normalize(update)
    d_update = norm_back(d_scaled, hat_out, inv_out)
    for part in range(ratio):
        grad_own[part] = jnp.concatenate(
            [
                d_update[i * cols + part * rows : i * cols + (part + 1) * rows]
                for i in range(rows)
            ],
            axis=0,
        ).astype(jnp.bfloat16)

    def grad_col_copy(part, to_col):
        return remote(
            grad_own.at[part],
            grad_col.at[row],
            grad_col_out.at[part * n_col + to_col],
            grad_col_in.at[row],
            col * ratio + part,
            to_col,
        )

    for part in range(ratio):

        def send_part(to_col, part=part):
            own = jnp.logical_and(col * ratio + part == row, to_col == col)

            @pl.when(jnp.logical_not(own))
            def _():
                grad_col_copy(part, to_col).start()

            @pl.when(own)
            def _():
                pltpu.make_async_copy(
                    grad_own.at[part], grad_col.at[row], grad_col_in.at[row]
                ).start()

        each(0, n_col, send_part)

    def grad_row_copy(step):
        slots = pl.ds(col * ratio, ratio)
        return remote(
            grad_own,
            grad_row.at[slots],
            grad_row_out.at[step],
            grad_row_in.at[col],
            row,
            lax.rem(col + step, n_col),
        )

    each(1, n_col, lambda step: grad_row_copy(step).start())
    grad_row[pl.ds(col * ratio, ratio)] = grad_own[...]

    mixed = (hat_out * gain_out + bias_out_ref[...]).astype(jnp.bfloat16)
    proj_out = dot(mixed, w_out_ref[...])
    d_gate_pre = (cot_full * proj_out * gating * (1.0 - gating)).astype(jnp.bfloat16)
    d_normed = dot_t(d_gate_pre, w_gate_ref[...])
    each(1, n_row, lambda step: arrived(right_panel, right_panel_in, lax.rem(row + step, n_row)))
    each(1, n_row, lambda step: arrived(left_panel, left_panel_in, lax.rem(row + step, n_row)))

    def grad_row_arrived(step):
        source = lax.rem(col + step, n_col)
        slots = pl.ds(source * ratio, ratio)
        remote(
            grad_row.at[slots],
            grad_row.at[slots],
            grad_row_in.at[source],
            grad_row_in.at[source],
            row,
            col,
        ).wait_recv()

    each(1, n_col, grad_row_arrived)
    grad_row_wide[...] = grad_row[...].astype(jnp.float32)

    def add_left(source, sums):
        sums = list(sums)
        panel = right_panel[source].astype(jnp.float32)
        for j in range(rows):
            panel_j = panel[j * cols : (j + 1) * cols]
            for i in range(rows):
                sums[i] += grad_row_wide[source, i * rows + j : i * rows + j + 1, :] * panel_j
        return tuple(sums)

    zero_wide = jnp.zeros((cols, width), jnp.float32)
    d_left = jnp.concatenate(loop(n_row, add_left, (zero_wide,) * rows), axis=0)
    left_part = d_left * pair_mask * left_sig
    d_left_pre = jnp.concatenate([left_part, left_part * left_lin * (1.0 - left_sig)], axis=1)
    d_normed += dot_t(d_left_pre.astype(jnp.bfloat16), w_left_ref[...])

    each(0, n_row, lambda slot: arrived(grad_col, grad_col_in, slot))
    grad_col_wide[...] = grad_col[...].astype(jnp.float32)

    def add_right(source, sums):
        sums = list(sums)
        panel = left_panel[source].astype(jnp.float32)
        for i in range(rows):
            panel_i = panel[i * cols : (i + 1) * cols]
            for j in range(rows):
                sums[j] += grad_col_wide[source, i * rows + j : i * rows + j + 1, :] * panel_i
        return tuple(sums)

    d_right = jnp.concatenate(loop(n_row, add_right, (zero_wide,) * rows), axis=0)
    right_part = d_right * pair_mask * right_sig
    d_right_pre = jnp.concatenate([right_part, right_part * right_lin * (1.0 - right_sig)], axis=1)
    d_normed += dot_t(d_right_pre.astype(jnp.bfloat16), w_right_ref[...])
    out_ref[...] = norm_back(d_normed * gain_in, hat_in, inv_in).astype(jnp.bfloat16)

    each(1, n_row, lambda step: turn_copy(step).wait_send())

    @pl.when(home_col != col)
    def _():
        turn_copy(0).wait_send()

    each(1, n_col, lambda step: left_row_copy(step).wait_send())
    each(1, n_row, lambda step: right_panel_copy(step).wait_send())
    each(1, n_row, lambda step: left_panel_copy(step).wait_send())
    each(1, n_col, lambda step: grad_row_copy(step).wait_send())
    for part in range(ratio):

        def sent_part(to_col, part=part):
            own = jnp.logical_and(col * ratio + part == row, to_col == col)

            @pl.when(jnp.logical_not(own))
            def _():
                grad_col_copy(part, to_col).wait_send()

        each(0, n_col, sent_part)


def solution(mesh):
    n_row = mesh.shape["row"]
    n_col = mesh.shape["col"]

    def shards(
        pair_act,
        cotangent,
        crop_len,
        ln_in_gain,
        ln_in_bias,
        w_left,
        w_right,
        w_gate,
        ln_out_gain,
        ln_out_bias,
        w_out,
    ):
        rows, cols, channels = pair_act.shape
        width = w_out.shape[0]
        ratio = cols // rows
        assert ratio * rows == cols and n_row * rows == n_col * cols
        cells, sub = rows * cols, rows * rows
        half, full, sems = jnp.bfloat16, jnp.float32, pltpu.SemaphoreType.DMA
        result = pl.pallas_call(
            functools.partial(kernel, n_row, n_col, rows, cols),
            out_shape=jax.ShapeDtypeStruct((cells, channels), half),
            in_specs=[pl.BlockSpec(memory_space=pltpu.HBM)] * 11,
            out_specs=pl.BlockSpec(memory_space=pltpu.VMEM),
            scratch_shapes=[
                pltpu.SMEM(crop_len.shape, jnp.int32),
                pltpu.VMEM((cells, channels), half),
                pltpu.VMEM((cells, channels), half),
                pltpu.VMEM((1, channels), full),
                pltpu.VMEM((1, channels), full),
                pltpu.VMEM(w_left.shape, half),
                pltpu.VMEM(w_right.shape, half),
                pltpu.VMEM(w_gate.shape, half),
                pltpu.VMEM((1, width), full),
                pltpu.VMEM((1, width), full),
                pltpu.VMEM(w_out.shape, half),
                sems((11,)),
                pltpu.VMEM((cells, width), half),
                pltpu.VMEM((cells, width), half),
                pltpu.VMEM((cells, width), half),
                pltpu.VMEM((ratio, sub, width), half),
                pltpu.VMEM((n_col, cells, width), half),
                pltpu.VMEM((ratio * n_col, cells, width), half),
                pltpu.VMEM((n_row, cells, width), half),
                pltpu.VMEM((n_row, cells, width), half),
                pltpu.VMEM((n_row, sub, width), half),
                pltpu.VMEM((n_row, sub, width), half),
                pltpu.VMEM((cells, width), full),
                pltpu.VMEM((n_col, cells, width), full),
                pltpu.VMEM((n_row, sub, width), full),
                pltpu.VMEM((n_row, sub, width), full),
                sems((n_col,)),
                sems((n_col,)),
                sems((n_row,)),
                sems((ratio * n_col,)),
                sems((n_row,)),
                sems((n_row,)),
                sems((n_row,)),
                sems((n_row,)),
                sems((n_col,)),
                sems((n_col,)),
                sems((ratio * n_col,)),
                sems((n_row,)),
            ],
            compiler_params=pltpu.CompilerParams(
                collective_id=0, has_side_effects=True, vmem_limit_bytes=60 * 1024 * 1024
            ),
        )(
            crop_len,
            pair_act.reshape(cells, channels),
            cotangent.reshape(cells, channels),
            ln_in_gain.reshape(1, channels),
            ln_in_bias.reshape(1, channels),
            w_left,
            w_right,
            w_gate,
            ln_out_gain.reshape(1, width),
            ln_out_bias.reshape(1, width),
            w_out,
        )
        return result.reshape(rows, cols, channels)

    pair_spec = P(("groups", "row"), "col", None)
    return jax.shard_map(
        shards,
        mesh=mesh,
        in_specs=(pair_spec, pair_spec, P("groups")) + (P(),) * 8,
        out_specs=pair_spec,
        check_vma=False,
    )
```

profile of v0, /device:TPU:0, one launch (start us, length us, event | category | flops | bytes accessed | tf_op | source)
XLA Modules:
  0.0 17.9 jit_solution(16078387783219067128)
XLA Ops:
  0.7 16.0 %shard_map.109 = bf16[64,128]{1,0:T(8,128)(2,1)} custom-call(s32[1]{0:T(128)S(6)} %copy.13.crop_hbm, bf16[64,128]{1,0:T(8,128)(2,1)} %bitcast.8, bf16[64,128]{1,0:T(8,128)(2,1)} %bitcast.9, f32[1,128]{1,0:T(1,128)} %bitcast.10, f32[1,128]{1,0:T(1,128)} %bitcast.11, bf16[128,256]{1,0:T(8,128)(2,1)} %w_left_hbm.1, bf16[128,256]{1,0:T(8,128)(2,1)} %w_right_hbm.1, ...), custom_call_target="tpu_custom_call" | custom-call | tf_op jit(solution)/shard_map/pallas_call | solution.py:430
  16.6 1.3 %copy.14 = bf16[8,8,128]{2,1,0:T(8,128)(2,1)} copy(bf16[8,8,128]{2,1,0:T(8,128)(2,1)} %bitcast.7) | data formatting | bytes 32768
where the time goes:
time: 18.3 us; the launch traced here: 17.9 us
  Pallas kernels  16 us (87%)
  local copies, waits for them, and re-layouts  1.32 us (7%)
  between operations  0.66 us (4%)
    pallas_call x1, Pallas kernels, shards(): pl.pallas_call(functools.partial(kernel, n_row, n_col, rows, cols), out_s...  16 us
    unnamed x1, local copies, waits for them, and re-layouts  1.32 us

commit v1 on v0

--- a/solution.py
+++ b/solution.py
@@ -80,14 +80,12 @@
     bias_out_ref,
     w_out_ref,
     load_in,
-    left_own,
-    right_own,
+    side_own,
     turn_own,
     grad_own,
     left_row,
     right_turn,
-    left_panel,
-    right_panel,
+    panel,
     grad_row,
     grad_col,
     right_wide,
@@ -98,10 +96,8 @@
     left_row_in,
     turn_out,
     turn_in,
-    left_panel_out,
-    left_panel_in,
-    right_panel_out,
-    right_panel_in,
+    panel_out,
+    panel_in,
     grad_row_out,
     grad_row_in,
     grad_col_out,
@@ -170,15 +166,11 @@
     right_lin = right_proj[:, :width]
     right_sig = jax.nn.sigmoid(right_proj[:, width:])
     right_side = (pair_mask * right_sig * right_lin).astype(jnp.bfloat16)
-    right_own[...] = right_side
+    side_own[1] = right_side
     right_wide[...] = right_side.astype(jnp.float32)
     turn_own[...] = jnp.concatenate(
         [right_wide[pl.ds(k, rows, stride=cols), :] for k in range(cols)], axis=0
     ).astype(jnp.bfloat16)
-    left_proj = dot(normed, w_left_ref[...])
-    left_lin = left_proj[:, :width]
-    left_sig = jax.nn.sigmoid(left_proj[:, width:])
-    left_own[...] = (pair_mask * left_sig * left_lin).astype(jnp.bfloat16)
 
     pl.semaphore_wait(barrier, total - 1)
 
@@ -204,9 +196,14 @@
     def _():
         pltpu.make_async_copy(turn_own, right_turn.at[turn_slot], turn_in.at[turn_slot]).start()
 
+    left_proj = dot(normed, w_left_ref[...])
+    left_lin = left_proj[:, :width]
+    left_sig = jax.nn.sigmoid(left_proj[:, width:])
+    side_own[0] = (pair_mask * left_sig * left_lin).astype(jnp.bfloat16)
+
     def left_row_copy(step):
         return remote(
-            left_own,
+            side_own.at[0],
             left_row.at[col],
             left_row_out.at[step],
             left_row_in.at[col],
@@ -216,32 +213,20 @@
 
     each(1, n_col, lambda step: left_row_copy(step).start())
 
-    def right_panel_copy(step):
+    def panel_copy(step):
         return remote(
-            right_own,
-            right_panel.at[row],
-            right_panel_out.at[step],
-            right_panel_in.at[row],
+            side_own,
+            panel.at[row],
+            panel_out.at[step],
+            panel_in.at[row],
             lax.rem(row + step, n_row),
             col,
         )
 
-    def left_panel_copy(step):
-        return remote(
-            left_own,
-            left_panel.at[row],
-            left_panel_out.at[step],
-            left_panel_in.at[row],
-            lax.rem(row + step, n_row),
-            col,
-        )
-
-    each(1, n_row, lambda step: right_panel_copy(step).start())
-    each(1, n_row, lambda step: left_panel_copy(step).start())
-
-    left_row[col] = left_own[...]
-    right_panel[row] = right_own[...]
-    left_panel[row] = left_own[...]
+    each(1, n_row, lambda step: panel_copy(step).start())
+
+    left_row[col] = side_own[0]
+    panel[row] = side_own[...]
 
     for load in loads[6:]:
         load.wait()
@@ -331,8 +316,7 @@
     proj_out = dot(mixed, w_out_ref[...])
     d_gate_pre = (cot_full * proj_out * gating * (1.0 - gating)).astype(jnp.bfloat16)
     d_normed = dot_t(d_gate_pre, w_gate_ref[...])
-    each(1, n_row, lambda step: arrived(right_panel, right_panel_in, lax.rem(row + step, n_row)))
-    each(1, n_row, lambda step: arrived(left_panel, left_panel_in, lax.rem(row + step, n_row)))
+    each(1, n_row, lambda step: arrived(panel, panel_in, lax.rem(row + step, n_row)))
 
     def grad_row_arrived(step):
         source = lax.rem(col + step, n_col)
@@ -351,11 +335,11 @@
 
     def add_left(source, sums):
         sums = list(sums)
-        panel = right_panel[source].astype(jnp.float32)
+        right = panel[source, 1].astype(jnp.float32)
         for j in range(rows):
-            panel_j = panel[j * cols : (j + 1) * cols]
+            right_j = right[j * cols : (j + 1) * cols]
             for i in range(rows):
-                sums[i] += grad_row_wide[source, i * rows + j : i * rows + j + 1, :] * panel_j
+                sums[i] += grad_row_wide[source, i * rows + j : i * rows + j + 1, :] * right_j
         return tuple(sums)
 
     zero_wide = jnp.zeros((cols, width), jnp.float32)
@@ -369,11 +353,11 @@
 
     def add_right(source, sums):
         sums = list(sums)
-        panel = left_panel[source].astype(jnp.float32)
+        left = panel[source, 0].astype(jnp.float32)
         for i in range(rows):
-            panel_i = panel[i * cols : (i + 1) * cols]
+            left_i = left[i * cols : (i + 1) * cols]
             for j in range(rows):
-                sums[j] += grad_col_wide[source, i * rows + j : i * rows + j + 1, :] * panel_i
+                sums[j] += grad_col_wide[source, i * rows + j : i * rows + j + 1, :] * left_i
         return tuple(sums)
 
     d_right = jnp.concatenate(loop(n_row, add_right, (zero_wide,) * rows), axis=0)
@@ -389,8 +373,7 @@
         turn_copy(0).wait_send()
 
     each(1, n_col, lambda step: left_row_copy(step).wait_send())
-    each(1, n_row, lambda step: right_panel_copy(step).wait_send())
-    each(1, n_row, lambda step: left_panel_copy(step).wait_send())
+    each(1, n_row, lambda step: panel_copy(step).wait_send())
     each(1, n_col, lambda step: grad_row_copy(step).wait_send())
     for part in range(ratio):
 
@@ -429,7 +412,7 @@
         half, full, sems = jnp.bfloat16, jnp.float32, pltpu.SemaphoreType.DMA
         result = pl.pallas_call(
             functools.partial(kernel, n_row, n_col, rows, cols),
-            out_shape=jax.ShapeDtypeStruct((cells, channels), half),
+            out_shape=pltpu.VMEM((cells, channels), half),
             in_specs=[pl.BlockSpec(memory_space=pltpu.HBM)] * 11,
             out_specs=pl.BlockSpec(memory_space=pltpu.VMEM),
             scratch_shapes=[
@@ -445,14 +428,12 @@
                 pltpu.VMEM((1, width), full),
                 pltpu.VMEM(w_out.shape, half),
                 sems((11,)),
-                pltpu.VMEM((cells, width), half),
-                pltpu.VMEM((cells, width), half),
+                pltpu.VMEM((2, cells, width), half),
                 pltpu.VMEM((cells, width), half),
                 pltpu.VMEM((ratio, sub, width), half),
                 pltpu.VMEM((n_col, cells, width), half),
                 pltpu.VMEM((ratio * n_col, cells, width), half),
-                pltpu.VMEM((n_row, cells, width), half),
-                pltpu.VMEM((n_row, cells, width), half),
+                pltpu.VMEM((n_row, 2, cells, width), half),
                 pltpu.VMEM((n_row, sub, width), half),
                 pltpu.VMEM((n_row, sub, width), half),
                 pltpu.VMEM((cells, width), full),
@@ -463,8 +444,6 @@
                 sems((n_col,)),
                 sems((n_row,)),
                 sems((ratio * n_col,)),
-                sems((n_row,)),
-                sems((n_row,)),
                 sems((n_row,)),
                 sems((n_row,)),
                 sems((n_col,)),

time: 18.3 us -> 16.8 us (0.918)
  local copies, waits for them, and re-layouts: 1.32 us -> 0.61 us
  Pallas kernels: 16 us -> 15.3 us
    unnamed x1, local copies, waits for them, and re-layouts: 1.32 us -> 0.61 us
    pallas_call x1, Pallas kernels: 16 us -> 15.3 us  [shards(): pl.pallas_call(functools.partial(kernel, n_row, n_col, rows, cols), out_s...]
where the time goes in v1:
time: 16.8 us; the launch traced here: 16.6 us
  Pallas kernels  15.3 us (91%)
  between operations  0.66 us (4%)
  local copies, waits for them, and re-layouts  0.61 us (4%)
    pallas_call x1, Pallas kernels, shards(): pl.pallas_call(functools.partial(kernel, n_row, n_col, rows, cols), out_s...  15.3 us
    unnamed x1, local copies, waits for them, and re-layouts  0.61 us

profile of v1, /device:TPU:0, one launch (start us, length us, event | category | flops | bytes accessed | tf_op | source)
XLA Modules:
  0.0 16.6 jit_solution(2552942471288534403)
XLA Ops:
  0.7 15.3 %shard_map.109 = bf16[64,128]{1,0:T(8,128)(2,1)S(1)} custom-call(s32[1]{0:T(128)S(6)} %copy.14.crop_hbm, bf16[64,128]{1,0:T(8,128)(2,1)} %bitcast.8, bf16[64,128]{1,0:T(8,128)(2,1)} %bitcast.9, f32[1,128]{1,0:T(1,128)} %bitcast.10, f32[1,128]{1,0:T(1,128)} %bitcast.11, bf16[128,256]{1,0:T(8,128)(2,1)} %w_left_hbm.1, bf16[128,256]{1,0:T(8,128)(2,1)} %w_right_hbm.1, ...), custom_call_target="tpu_custom_call" | custom-call | tf_op jit(solution)/shard_map/pallas_call | solution.py:413
  16.0 0.6 %copy.13 = bf16[8,8,128]{2,1,0:T(8,128)(2,1)} copy(bf16[8,8,128]{2,1,0:T(8,128)(2,1)S(1)} %bitcast.7) | data formatting | bytes 32768

commit v2 on v1

--- a/solution.py
+++ b/solution.py
@@ -114,24 +114,13 @@
 
     barrier = pltpu.get_barrier_semaphore()
 
-    def greet(step):
-        other = lax.rem(row * n_col + col + step, total)
-        pl.semaphore_signal(
-            barrier,
-            inc=1,
-            device_id={"row": other // n_col, "col": lax.rem(other, n_col)},
-            device_id_type=MESH,
-        )
-
-    each(1, total, greet)
-
     pairs = (
         (pair_hbm, pair_ref),
         (gain_in_hbm, gain_in_ref),
         (bias_in_hbm, bias_in_ref),
         (w_right_hbm, w_right_ref),
+        (crop_hbm, crop_ref),
         (w_left_hbm, w_left_ref),
-        (crop_hbm, crop_ref),
         (w_gate_hbm, w_gate_ref),
         (cot_hbm, cot_ref),
         (w_out_hbm, w_out_ref),
@@ -139,7 +128,29 @@
         (bias_out_hbm, bias_out_ref),
     )
     loads = [pltpu.make_async_copy(*pair, load_in.at[at]) for at, pair in enumerate(pairs)]
-    for load in loads:
+    for load in loads[:5]:
+        load.start()
+
+    def greet(step):
+        other = lax.rem(row * n_col + col + step, total)
+        other_row, other_col = other // n_col, lax.rem(other, n_col)
+        same_row = jnp.logical_or(other_row == row, other_row // ratio == col)
+        same_col = jnp.logical_or(other_col == col, other_col == home_col)
+
+        @pl.when(jnp.logical_or(same_row, same_col))
+        def _():
+            pl.semaphore_signal(
+                barrier,
+                inc=1,
+                device_id={"row": other_row, "col": other_col},
+                device_id_type=MESH,
+            )
+
+    each(1, total, greet)
+    apart = (home_col != col).astype(jnp.int32)
+    row_count, col_count = ratio + apart, 1 + apart
+    greeted = row_count * n_col + col_count * n_row - row_count * col_count - 1
+    for load in loads[5:]:
         load.start()
 
     def remote(src, dst, out_sem, in_sem, to_row, to_col):
@@ -152,7 +163,7 @@
             device_id_type=MESH,
         )
 
-    for load in loads[:6]:
+    for load in loads[:5]:
         load.wait()
     position = (rows, cols, width)
     row_pos = row * rows + lax.broadcasted_iota(jnp.int32, position, 0)
@@ -172,7 +183,7 @@
         [right_wide[pl.ds(k, rows, stride=cols), :] for k in range(cols)], axis=0
     ).astype(jnp.bfloat16)
 
-    pl.semaphore_wait(barrier, total - 1)
+    pl.semaphore_wait(barrier, greeted)
 
     turn_slot = lax.rem(row, ratio) * n_col + col
 
@@ -196,6 +207,7 @@
     def _():
         pltpu.make_async_copy(turn_own, right_turn.at[turn_slot], turn_in.at[turn_slot]).start()
 
+    loads[5].wait()
     left_proj = dot(normed, w_left_ref[...])
     left_lin = left_proj[:, :width]
     left_sig = jax.nn.sigmoid(left_proj[:, width:])

time: 16.8 us -> 16.9 us (level)
  no operation moved by 1% of the time
where the time goes in v2:
time: 16.9 us; the launch traced here: 16.6 us
  Pallas kernels  15.3 us (91%)
  between operations  0.66 us (4%)
  local copies, waits for them, and re-layouts  0.61 us (4%)
    pallas_call x1, Pallas kernels, shards(): pl.pallas_call(functools.partial(kernel, n_row, n_col, rows, cols), out_s...  15.3 us
    unnamed x1, local copies, waits for them, and re-layouts  0.61 us

profile of v2, /device:TPU:0, one launch (start us, length us, event | category | flops | bytes accessed | tf_op | source)
XLA Modules:
  0.0 16.6 jit_solution(12144844033797096727)
XLA Ops:
  0.7 15.3 %shard_map.109 = bf16[64,128]{1,0:T(8,128)(2,1)S(1)} custom-call(s32[1]{0:T(128)S(6)} %copy.14.crop_hbm, bf16[64,128]{1,0:T(8,128)(2,1)} %bitcast.8, bf16[64,128]{1,0:T(8,128)(2,1)} %bitcast.9, f32[1,128]{1,0:T(1,128)} %bitcast.10, f32[1,128]{1,0:T(1,128)} %bitcast.11, bf16[128,256]{1,0:T(8,128)(2,1)} %w_left_hbm.1, bf16[128,256]{1,0:T(8,128)(2,1)} %w_right_hbm.1, ...), custom_call_target="tpu_custom_call" | custom-call | tf_op jit(solution)/shard_map/pallas_call | solution.py:425
  16.0 0.6 %copy.13 = bf16[8,8,128]{2,1,0:T(8,128)(2,1)} copy(bf16[8,8,128]{2,1,0:T(8,128)(2,1)S(1)} %bitcast.7) | data formatting | bytes 32768
